TPU v7x, 256 devices: a whole 4x4x8 slice. The times are simulated.
256 devices in a mesh: chan: 16 (over y, x_hi, core), seg: 16 (over x_lo, z).
Axes of the slice: x: 4 (x_hi: 2, x_lo: 2; x = x_hi * 2 + x_lo), y: 4, z: 8, core: 2. Of those that a mesh axis runs over, the one named last changes fastest.
Arguments:
- samples: bfloat16 [4096, 240, 1024], P('chan', 'seg'), may hold values from -1000 to 1000
- live_trace: int32 [4096], P('chan'), may hold values 0 or 1
Outputs:
- stacked: bfloat16 [64, 4096, 5, 512], P('seg', 'chan')
All inputs are finite; a program needn't handle non-finite values. No bound on the sum of `live_trace` on one device may be relied on, other than what follows from the above.
Results may differ from a plain program's by a relative error of at most 0.0057.
Values may be sent and summed in bfloat16 or wider, within the bound.
A program may use at most 64 MiB of HBM per device.

v0:
```python
import math

import jax
import jax.numpy as jnp
from jax import lax
from jax.sharding import PartitionSpec as P

L = 1024
F = 64
F0 = 16
REACH = 4
NEAR = 5


eps_power = 1e-06
water_level = 0.1
smooth_half = 2


def shifted(block, axis, distance):
    devices = range(lax.axis_size(axis))
    route = [(i - distance, i) for i in devices if i - distance in devices]
    return lax.ppermute(block, axis, route)


def dft_table(length, first, bins):
    sample_index = jnp.arange(length, dtype=jnp.int32)
    bin_number = jnp.arange(bins, dtype=jnp.int32) + first
    phase_step = (sample_index[:, None] * bin_number[None, :] % length).astype(jnp.float32)
    angle_value = phase_step * (2.0 * math.pi / length)
    window_taper = 0.5 - 0.5 * jnp.cos(sample_index.astype(jnp.float32) * (2.0 * math.pi / length))
    stacked_table = jnp.stack(
        [
            window_taper[:, None] * jnp.cos(angle_value),
            -window_taper[:, None] * jnp.sin(angle_value),
        ],
        axis=-1,
    )
    return stacked_table.reshape(length, 2 * bins).astype(jnp.bfloat16)


def smoother(bins):
    bin_index = jnp.arange(bins, dtype=jnp.int32)
    in_window = (jnp.abs(bin_index[:, None] - bin_index[None, :]) <= smooth_half).astype(
        jnp.float32
    )
    return in_window / jnp.sum(in_window, axis=0, keepdims=True)


def cross_block(own_band, partner_band):
    band_bins, parts, seg_total, width = own_band.shape
    own_rows = own_band.reshape(band_bins, parts * seg_total, width)
    partner_real = partner_band[:, 0]
    partner_imag = partner_band[:, 1]
    upper_half = jnp.concatenate([partner_real, partner_imag], axis=-1)
    lower_half = jnp.concatenate([partner_imag, -partner_real], axis=-1)
    partner_rows = jnp.concatenate([upper_half, lower_half], axis=1)
    return jnp.einsum("fkc,fkm->fcm", own_rows, partner_rows, preferred_element_type=jnp.float32)


def on_device(samples, live_trace):
    channels_here = samples.shape[0]
    seg_here = samples.shape[1]
    length = samples.shape[2]
    transform_table = dft_table(L, F0, F)
    alive_mask = live_trace.astype(jnp.float32)
    spectra = jnp.einsum(
        "csl,lq->qsc", samples, transform_table, preferred_element_type=jnp.float32
    ).reshape(F, 2, seg_here, channels_here)
    energy = jnp.einsum("csl,csl->cs", samples, samples, preferred_element_type=jnp.float32)
    local_power = jnp.sum(alive_mask[:, None] * energy, axis=0)
    all_channels = channels_here * lax.axis_size("chan")
    power_sum = lax.psum(local_power, "chan")
    weights = 1.0 / jnp.sqrt(power_sum / (all_channels * length) + eps_power)
    weight_total = lax.psum(jnp.sum(weights), "seg")
    power_level = spectra[:, 0] * spectra[:, 0] + spectra[:, 1] * spectra[:, 1]
    smooth = jnp.einsum("gf,gsc->fsc", smoother(F), power_level, precision=lax.Precision.HIGHEST)
    denominator = jnp.sqrt(
        smooth + water_level * jnp.mean(power_level, axis=0, keepdims=True) + eps_power
    )
    gain_value = alive_mask[None, None, :] * jnp.sqrt(weights)[None, :, None] / denominator
    whitened = (spectra * gain_value[:, None]).astype(jnp.bfloat16)
    banded = lax.all_to_all(whitened, "seg", split_axis=0, concat_axis=2, tiled=True)
    seg_total = banded.shape[2]
    factor = math.sqrt(seg_total) / weight_total
    row_index = jnp.arange(channels_here, dtype=jnp.int32)
    offsets = jnp.arange(NEAR, dtype=jnp.int32)
    distance = offsets[:, None] * channels_here + row_index[None, :]
    distance = distance[None, :, :] - row_index[:, None, None]
    half_mask = ((distance > 0) & (distance <= REACH * channels_here)).astype(jnp.float32)
    pair_mask = jnp.concatenate([half_mask, half_mask], axis=-1)
    products = [cross_block(banded, banded)]
    moving = banded
    for offset in range(1, REACH + 1):
        moving = shifted(moving, "chan", -1)
        products.append(cross_block(banded, moving))
    combined = jnp.stack(products, axis=2)
    return (combined * (factor * pair_mask)[None]).astype(jnp.bfloat16)


def solution(mesh):
    in_specs = (P("chan", "seg", None), P("chan"))
    out_specs = P("seg", "chan", None, None)
    return jax.shard_map(
        on_device, mesh=mesh, in_specs=in_specs, out_specs=out_specs, check_vma=False
    )
```

profile of v0, /device:TPU:7, one launch (start us, length us, event | category | flops | bytes accessed | tf_op | source)
XLA Modules:
  0.0 185.1 jit_solution(5494531366251129)
XLA Ops:
  0.1 0.1 convert_reduce_fusion
  0.2 1.2 multiply_convert_fusion.2
  1.4 0.3 copy.91
  1.7 0.1 reshape.254
  1.8 0.0 copy-start
  1.8 5.0 %fusion = f32[256,15]{0,1:T(8,128)S(1)} fusion(bf16[256,15,1024]{2,0,1:T(8,128)(2,1)} %param.2), kind=kLoop, calls=%fused_computation.1 | loop fusion | flops 11792640 | bytes 7879680 | tf_op jit(solution)/shard_map/csl,csl->cs/dot_general | solution.py:70
  6.8 0.5 copy-done
  7.3 4.0 %convolution_bitcast_fusion = f32[128,15,256]{2,0,1:T(8,128)} fusion(bf16[1024,128,1]{0,1,2:T(8,128)(2,1)S(1)} %reshape.254, bf16[256,15,1024]{2,0,1:T(8,128)(2,1)S(1)} %copy-done), kind=kOutput, calls=%fused_computation.51 | convolution fusion | flops 1006632960 | bytes 10092544 | tf_op jit(solution)/shard_map/csl,lq->qsc/dot_general | solution.py:67
  11.3 0.0 copy-start.1
  11.3 2.5 %reshape.252 = f32[64,2,15,256]{3,1,0,2:T(2,128)S(1)} reshape(f32[128,15,256]{2,0,1:T(8,128)} %convolution_bitcast_fusion) | data formatting | bytes 3932160 | tf_op jit(solution)/shard_map/reshape | solution.py:69
  13.8 1.9 %fusion.90 = (f32[15,256]{1,0:T(8,128)S(1)}, f32[64,1,15,256]{3,1,0,2:T(1,128)S(1)}) fusion(f32[64,2,15,256]{3,1,0,2:T(2,128)S(1)} %reshape.252), kind=kLoop, calls=%fused_computation.120 | loop fusion | flops 979200 | bytes 2964480 | tf_op jit(solution)/shard_map/reduce_sum | solution.py:79
  15.6 0.0 copy-done.1
  15.7 0.1 multiply_reduce_fusion
  15.8 28.7 %psum.14 = f32[15]{0:T(128)S(1)} all-reduce(f32[15]{0:T(128)S(1)} %multiply_reduce_fusion), channel_id=1, replica_groups=mesh['chan'=16,'seg'=16] {'chan'}, use_global_device_ids=true, to_apply=%region_1.2 | all-reduce | flops 15 | bytes 120 | tf_op jit(solution)/shard_map/psum | solution.py:73
  44.5 0.6 fusion.83
  45.1 0.1 broadcast_multiply_fusion.1
  45.2 1.0 fusion.54
  46.2 0.4 fusion.41
  46.6 1.0 copy.93
  47.6 27.5 %all_to_all.18 = bf16[64,2,15,256]{3,1,2,0:T(2,128)(2,1)S(1)} all-to-all(bf16[64,2,15,256]{3,1,2,0:T(2,128)(2,1)S(1)} %copy.93), channel_id=1, replica_groups=mesh['chan'=16,'seg'=16] {'seg'}, dimensions={0} | all-to-all | bytes 1966080 | tf_op jit(solution)/shard_map/all_to_all | solution.py:83
  75.1 0.7 copy.95
  75.8 0.1 copy.96
  76.0 9.4 %collective-permute-start = (bf16[4,2,240,256]{3,2,0,1:T(8,128)(2,1)S(1)}, bf16[4,2,240,256]{3,2,0,1:T(8,128)(2,1)S(1)}, u32[]{:S(2)}, u32[]{:S(2)}) collective-permute-start(bf16[4,2,240,256]{3,2,0,1:T(8,128)(2,1)S(1)} %copy.96), channel_id=1, source_target_pairs={{16,0},{32,16},{48,32},{64,48},{80,64},{96,80},{112,96},{128,112},... | collective-permute-start | bytes 2949128 | tf_op jit(solution)/shard_map/ppermute | solution.py:23
  85.4 27.3 %psum.15 = f32[]{:T(128)} all-reduce(f32[]{:T(128)} %get-tuple-element.17), channel_id=1, replica_groups=mesh['chan'=16,'seg'=16] {'seg'}, use_global_device_ids=true, to_apply=%region_5.6 | all-reduce | flops 1 | bytes 8 | tf_op jit(solution)/shard_map/psum | solution.py:75
  113.4 0.1 iota_add_fusion
  113.5 0.3 fusion.57
  113.8 1.9 %add_select_fusion = f32[256,5,512]{2,0,1:T(8,128)} fusion(pred[256,5,256]{2,0,1:T(8,128)(4,1)S(1)} %fusion.57, f32[]{:T(128)S(6)} %div.30), kind=kLoop, calls=%fused_computation.3 | loop fusion | flops 1310720 | bytes 2949124 | tf_op jit(solution)/shard_map/mul | solution.py:98
  115.6 0.0 collective-permute-done
  115.6 9.1 %collective-permute-start.1 = (bf16[4,2,240,256]{3,2,0,1:T(8,128)(2,1)S(1)}, bf16[4,2,240,256]{3,2,0,1:T(8,128)(2,1)S(1)}, u32[]{:S(2)}, u32[]{:S(2)}) collective-permute-start(bf16[4,2,240,256]{3,2,0,1:T(8,128)(2,1)S(1)} %collective-permute-done), channel_id=1, source_target_pairs={{16,0},{32,16},{48,32},{64,48},{80,64},{96,80},{112,96},{128,112},... | collective-permute-start | bytes 2949128 | tf_op jit(solution)/shard_map/ppermute | solution.py:23
  124.8 0.4 copy.94
  125.2 0.1 slice_bitcast_fusion.9
  125.3 2.1 %bitcast_dynamic-update-slice_fusion.4 = f32[4,256,5,512]{3,1,0,2:T(8,128)} fusion(bf16[4,240,256]{2,1,0:T(8,128)(2,1)S(1)} %fusion.85, bf16[4,240,256]{2,1,0:T(8,128)(2,1)S(1)} %get-tuple-element.16, bf16[4,240,256]{2,1,0:T(8,128)(2,1)S(1)} %get-tuple-element.15, bf16[4,480,256]{2,0,1:T(4,128)(2,1)S(1)} %bitcast.62), kind=kOutput, calls=%fused_computation.8 | convolution fusion | flops 511180800 | bytes 4554752 | tf_op jit(solution)/shard_map/fkc,fkm->fcm/dot_general | solution.py:58
  127.4 0.1 slice_bitcast_fusion.7
  127.5 10.3 %collective-permute-done.1 = bf16[4,2,240,256]{3,2,0,1:T(8,128)(2,1)S(1)} collective-permute-done((bf16[4,2,240,256]{3,2,0,1:T(8,128)(2,1)S(1)}, bf16[4,2,240,256]{3,2,0,1:T(8,128)(2,1)S(1)}, u32[]{:S(2)}, u32[]{:S(2)}) %collective-permute-start.1) | collective-permute-done | bytes 983072 | tf_op jit(solution)/shard_map/ppermute | solution.py:23
  137.7 1.9 %collective-permute-start.2 = (bf16[4,2,240,256]{3,2,0,1:T(8,128)(2,1)S(1)}, bf16[4,2,240,256]{3,2,0,1:T(8,128)(2,1)S(1)}, u32[]{:S(2)}, u32[]{:S(2)}) collective-permute-start(bf16[4,2,240,256]{3,2,0,1:T(8,128)(2,1)S(1)} %collective-permute-done.1), channel_id=1, source_target_pairs={{16,0},{32,16},{48,32},{64,48},{80,64},{96,80},{112,96},{128,112},... | collective-permute-start | bytes 2949128 | tf_op jit(solution)/shard_map/ppermute | solution.py:23
  139.7 2.0 %bitcast_dynamic-update-slice_fusion.3 = f32[4,256,5,512]{3,1,0,2:T(8,128)} fusion(f32[4,256,5,512]{3,1,0,2:T(8,128)} %bitcast_dynamic-update-slice_fusion.4, bf16[4,240,256]{2,1,0:T(8,128)(2,1)S(1)} %fusion.86, bf16[4,240,256]{2,1,0:T(8,128)(2,1)S(1)} %get-tuple-element.14, bf16[4,240,256]{2,1,0:T(8,128)(2,1)S(1)} %get-tuple-element.13, ...), kind=kOutput, calls=%fused_computation.7 | convolution fusion | flops 511180800 | bytes 4554752 | tf_op jit(solution)/shard_map/fkc,fkm->fcm/dot_general | solution.py:58
  141.8 0.1 slice_bitcast_fusion.5
  141.9 13.7 %collective-permute-done.2 = bf16[4,2,240,256]{3,2,0,1:T(8,128)(2,1)S(1)} collective-permute-done((bf16[4,2,240,256]{3,2,0,1:T(8,128)(2,1)S(1)}, bf16[4,2,240,256]{3,2,0,1:T(8,128)(2,1)S(1)}, u32[]{:S(2)}, u32[]{:S(2)}) %collective-permute-start.2) | collective-permute-done | bytes 983072 | tf_op jit(solution)/shard_map/ppermute | solution.py:23
  155.6 1.9 %collective-permute-start.3 = (bf16[4,2,240,256]{3,2,0,1:T(8,128)(2,1)S(1)}, bf16[4,2,240,256]{3,2,0,1:T(8,128)(2,1)S(1)}, u32[]{:S(2)}, u32[]{:S(2)}) collective-permute-start(bf16[4,2,240,256]{3,2,0,1:T(8,128)(2,1)S(1)} %collective-permute-done.2), channel_id=1, source_target_pairs={{16,0},{32,16},{48,32},{64,48},{80,64},{96,80},{112,96},{128,112},... | collective-permute-start | bytes 2949128 | tf_op jit(solution)/shard_map/ppermute | solution.py:23
  157.5 2.1 %bitcast_dynamic-update-slice_fusion.2 = f32[4,256,5,512]{3,1,0,2:T(8,128)} fusion(f32[4,256,5,512]{3,1,0,2:T(8,128)} %bitcast_dynamic-update-slice_fusion.3, bf16[4,240,256]{2,1,0:T(8,128)(2,1)S(1)} %fusion.87, bf16[4,240,256]{2,1,0:T(8,128)(2,1)S(1)} %get-tuple-element.12, bf16[4,240,256]{2,1,0:T(8,128)(2,1)S(1)} %get-tuple-element.11, ...), kind=kOutput, calls=%fused_computation.6 | convolution fusion | flops 511180800 | bytes 4554752 | tf_op jit(solution)/shard_map/fkc,fkm->fcm/dot_general | solution.py:58
  159.6 0.1 slice_bitcast_fusion.3
  159.7 2.1 %bitcast_dynamic-update-slice_fusion.1 = f32[4,256,5,512]{3,1,0,2:T(8,128)} fusion(f32[4,256,5,512]{3,1,0,2:T(8,128)} %bitcast_dynamic-update-slice_fusion.2, bf16[4,240,256]{2,1,0:T(8,128)(2,1)S(1)} %fusion.88, bf16[4,240,256]{2,1,0:T(8,128)(2,1)S(1)} %get-tuple-element.10, bf16[4,240,256]{2,1,0:T(8,128)(2,1)S(1)} %get-tuple-element.9, ...), kind=kOutput, calls=%fused_computation.5 | convolution fusion | flops 511180800 | bytes 4554752 | tf_op jit(solution)/shard_map/fkc,fkm->fcm/dot_general | solution.py:58
  161.8 11.6 %collective-permute-done.3 = bf16[4,2,240,256]{3,2,0,1:T(8,128)(2,1)S(1)} collective-permute-done((bf16[4,2,240,256]{3,2,0,1:T(8,128)(2,1)S(1)}, bf16[4,2,240,256]{3,2,0,1:T(8,128)(2,1)S(1)}, u32[]{:S(2)}, u32[]{:S(2)}) %collective-permute-start.3) | collective-permute-done | bytes 983072 | tf_op jit(solution)/shard_map/ppermute | solution.py:23
  173.4 0.1 slice_bitcast_fusion.1
  173.5 2.1 %bitcast_dynamic-update-slice_fusion = f32[4,256,5,512]{3,1,0,2:T(8,128)} fusion(f32[4,256,5,512]{3,1,0,2:T(8,128)} %bitcast_dynamic-update-slice_fusion.1, bf16[4,240,256]{2,1,0:T(8,128)(2,1)S(1)} %fusion.89, bf16[4,240,256]{2,1,0:T(8,128)(2,1)S(1)} %get-tuple-element.8, bf16[4,240,256]{2,1,0:T(8,128)(2,1)S(1)} %get-tuple-element.7, ...), kind=kOutput, calls=%fused_computation.4 | convolution fusion | flops 511180800 | bytes 4554752 | tf_op jit(solution)/shard_map/fkc,fkm->fcm/dot_general | solution.py:58
  175.6 6.6 %multiply_convert_fusion = bf16[4,256,5,512]{3,1,0,2:T(8,128)(2,1)S(1)} fusion(f32[4,256,5,512]{3,1,0,2:T(8,128)} %bitcast_dynamic-update-slice_fusion, f32[256,5,512]{2,0,1:T(8,128)} %add_select_fusion), kind=kLoop, calls=%fused_computation.2 | loop fusion | flops 5242880 | bytes 18350080 | tf_op jit(solution)/shard_map/convert_element_type | solution.py:98
  182.3 2.9 %copy.104 = bf16[4,256,5,512]{3,1,2,0:T(8,128)(2,1)} copy(bf16[4,256,5,512]{3,1,0,2:T(8,128)(2,1)S(1)} %multiply_convert_fusion) | data formatting | bytes 10485760 | tf_op jit(solution)/shard_map/convert_element_type | solution.py:98
  (11 shorter events, 0.3 us)
Async XLA Ops:
  1.8 5.5 %copy-start = (bf16[256,15,1024]{2,0,1:T(8,128)(2,1)S(1)}, bf16[256,15,1024]{2,0,1:T(8,128)(2,1)}, u32[]{:S(2)}) copy-start(bf16[256,15,1024]{2,0,1:T(8,128)(2,1)} %param.2) | copy-start | bytes 23592964
  11.3 4.4 %copy-start.1 = (s32[256]{0:T(256)S(1)}, s32[256]{0:T(256)}, u32[]{:S(2)}) copy-start(s32[256]{0:T(256)} %param.3) | copy-start | bytes 3076
  76.0 39.7 %collective-permute-start = (bf16[4,2,240,256]{3,2,0,1:T(8,128)(2,1)S(1)}, bf16[4,2,240,256]{3,2,0,1:T(8,128)(2,1)S(1)}, u32[]{:S(2)}, u32[]{:S(2)}) collective-permute-start(bf16[4,2,240,256]{3,2,0,1:T(8,128)(2,1)S(1)} %copy.96), channel_id=1, source_target_pairs={{16,0},{32,16},{48,32},{64,48},{80,64},{96,80},{112,96},{128,112},... | collective-permute-start | bytes 2949128 | tf_op jit(solution)/shard_map/ppermute | solution.py:23
  115.6 22.1 %collective-permute-start.1 = (bf16[4,2,240,256]{3,2,0,1:T(8,128)(2,1)S(1)}, bf16[4,2,240,256]{3,2,0,1:T(8,128)(2,1)S(1)}, u32[]{:S(2)}, u32[]{:S(2)}) collective-permute-start(bf16[4,2,240,256]{3,2,0,1:T(8,128)(2,1)S(1)} %collective-permute-done), channel_id=1, source_target_pairs={{16,0},{32,16},{48,32},{64,48},{80,64},{96,80},{112,96},{128,112},... | collective-permute-start | bytes 2949128 | tf_op jit(solution)/shard_map/ppermute | solution.py:23
  137.7 17.8 %collective-permute-start.2 = (bf16[4,2,240,256]{3,2,0,1:T(8,128)(2,1)S(1)}, bf16[4,2,240,256]{3,2,0,1:T(8,128)(2,1)S(1)}, u32[]{:S(2)}, u32[]{:S(2)}) collective-permute-start(bf16[4,2,240,256]{3,2,0,1:T(8,128)(2,1)S(1)} %collective-permute-done.1), channel_id=1, source_target_pairs={{16,0},{32,16},{48,32},{64,48},{80,64},{96,80},{112,96},{128,112},... | collective-permute-start | bytes 2949128 | tf_op jit(solution)/shard_map/ppermute | solution.py:23
  155.6 17.8 %collective-permute-start.3 = (bf16[4,2,240,256]{3,2,0,1:T(8,128)(2,1)S(1)}, bf16[4,2,240,256]{3,2,0,1:T(8,128)(2,1)S(1)}, u32[]{:S(2)}, u32[]{:S(2)}) collective-permute-start(bf16[4,2,240,256]{3,2,0,1:T(8,128)(2,1)S(1)} %collective-permute-done.2), channel_id=1, source_target_pairs={{16,0},{32,16},{48,32},{64,48},{80,64},{96,80},{112,96},{128,112},... | collective-permute-start | bytes 2949128 | tf_op jit(solution)/shard_map/ppermute | solution.py:23
where the time goes:
time: 187 us; the launch traced here: 185 us
  blocking collectives  83.5 us (45%)
  waiting for transfers between devices  35.6 us (19%)
  starting transfers between devices  22.4 us (12%)
  other arithmetic  18.5 us (10%)
  matrix products  15.5 us (8%)
  local copies, waits for them, and re-layouts  8.74 us (5%)
    ppermute x4, waiting for transfers between devices, shifted(): return lax.ppermute(block, axis, route)  35.6 us
    psum x1, blocking collectives, on_device(): power_sum = lax.psum(local_power, 'chan')  28.7 us
    all_to_all x1, blocking collectives, on_device(): lax.all_to_all(whitened, 'seg', split_axis=0, concat_axis=2, tiled=True)  27.5 us
    psum x1, blocking collectives, on_device(): weight_total = lax.psum(jnp.sum(weights), 'seg')  27.3 us
    ppermute x4, starting transfers between devices, shifted(): return lax.ppermute(block, axis, route)  22.4 us
    dot_general x5, matrix products, cross_block(): jnp.einsum('fkc,fkm->fcm', own_rows, partner_rows, preferred_element_type...  10.5 us
    convert_element_type x1, other arithmetic, on_device(): return (combined * (factor * pair_mask)[None]).astype(jnp.bfloat16)  6.64 us
    dot_general x1, other arithmetic, on_device(): jnp.einsum('csl,csl->cs', samples, samples, preferred_element_type=jnp.fl...  4.99 us
  transfers between devices with their start and end apart: 4, of which 3 were waited for; matrix products, arithmetic and copies ran while one was open for 6% of the time, Pallas kernels for 0%

commit v1 on v0

v1 whole, which is shorter than its diff:
```python
import functools
import math

import jax
import jax.numpy as jnp
import numpy as np
from jax import lax
from jax.experimental import pallas as pl
from jax.experimental.pallas import tpu as pltpu
from jax.sharding import PartitionSpec as P

L = 1024
F = 64
F0 = 16
REACH = 4
NEAR = 5
CH = 256
CHANNELS = 4096
SEGMENTS = 240
N_CHAN = 16
N_SEG = 16
SEG_DEV = 15
SEG_PAD = 16
BAND = F // N_SEG
STEP = 3

eps_power = 1e-06
water_level = 0.1
smooth_half = 2

MESH = pl.DeviceIdType.MESH


def dft_table():
    time_index = np.arange(L)
    bin_number = np.arange(F) + F0
    phase_step = (time_index[:, None] * bin_number[None, :] % L).astype(np.float32)
    angle = phase_step * np.float32(2.0 * math.pi / L)
    taper = np.float32(0.5) - np.float32(0.5) * np.cos(
        time_index.astype(np.float32) * np.float32(2.0 * math.pi / L)
    )
    real = taper[:, None] * np.cos(angle)
    imag = -taper[:, None] * np.sin(angle)
    return np.concatenate([real, imag], axis=1).astype(jnp.bfloat16)


def inverse_counts():
    bins = np.arange(F)
    count = np.minimum(bins, smooth_half) + np.minimum(F - 1 - bins, smooth_half) + 1
    return np.broadcast_to((1.0 / count).astype(np.float32)[:, None], (F, CH)).copy()


def whiten_kernel(x_ref, table_ref, row_ref, col_ref, count_ref, out_ref, power_ref, wide, padded):
    step = pl.program_id(0)
    lane = lax.broadcasted_iota(jnp.int32, (1, 128), 1)

    @pl.when(step == 0)
    def _():
        power_ref[...] = jnp.zeros_like(power_ref)
        padded[...] = jnp.zeros_like(padded)
        for half in range(2):
            wide[half, SEG_DEV * 2 * F :, :] = jnp.zeros((2 * F, 128), jnp.float32)

    for j in range(STEP):
        seg = step * STEP + j
        x = x_ref[j]
        spectra = jnp.dot(x, table_ref[...], preferred_element_type=jnp.float32)
        squares = jnp.zeros((CH, 128), jnp.float32)
        for tile in range(L // 128):
            part = x[:, tile * 128 : (tile + 1) * 128].astype(jnp.float32)
            squares += part * part
        total = jnp.sum(squares * col_ref[...])
        power_ref[...] += jnp.where(lane == seg, total, 0.0)
        spectra = spectra.T
        real = spectra[:F]
        imag = spectra[F:]
        level = real * real + imag * imag
        padded[8 : 8 + F, :] = level
        near = level
        for distance in (-2, -1, 1, 2):
            near += padded[8 + distance : 8 + distance + F, :]
        mean = jnp.sum(level, axis=0, keepdims=True) * (water_level / F)
        gain = row_ref[...] / jnp.sqrt(near * count_ref[...] + mean + eps_power)
        real = real * gain
        imag = imag * gain
        base = pl.multiple_of(seg * 2 * F, 2 * F)
        for half in range(2):
            lanes = slice(half * 128, half * 128 + 128)
            wide[half, pl.ds(base, F), :] = real[:, lanes]
            wide[half, pl.ds(base + F, F), :] = imag[:, lanes]

    @pl.when(step == SEG_DEV // STEP - 1)
    def _():
        for bin_number in range(F):
            for r in range(2):
                for half in range(2):
                    rows = wide[half, pl.ds(r * F + bin_number, SEG_PAD, stride=2 * F), :]
                    out_ref[
                        bin_number // BAND,
                        bin_number % BAND,
                        r * SEG_PAD : (r + 1) * SEG_PAD,
                        half * 128 : half * 128 + 128,
                    ] = rows.astype(jnp.bfloat16)


def whiten(samples, live):
    return pl.pallas_call(
        whiten_kernel,
        grid=(SEG_DEV // STEP,),
        out_shape=(
            jax.ShapeDtypeStruct((N_SEG, BAND, 2 * SEG_PAD, CH), jnp.bfloat16),
            jax.ShapeDtypeStruct((1, 128), jnp.float32),
        ),
        in_specs=[
            pl.BlockSpec((STEP, CH, L), lambda i: (i, 0, 0)),
            pl.BlockSpec((L, 2 * F), lambda i: (0, 0)),
            pl.BlockSpec((1, CH), lambda i: (0, 0)),
            pl.BlockSpec((CH, 1), lambda i: (0, 0)),
            pl.BlockSpec((F, CH), lambda i: (0, 0)),
        ],
        out_specs=(
            pl.BlockSpec((N_SEG, BAND, 2 * SEG_PAD, CH), lambda i: (0, 0, 0, 0)),
            pl.BlockSpec((1, 128), lambda i: (0, 0)),
        ),
        scratch_shapes=[
            pltpu.VMEM((2, SEG_PAD * 2 * F, 128), jnp.float32),
            pltpu.VMEM((F + 16, CH), jnp.float32),
        ],
        compiler_params=pltpu.CompilerParams(vmem_limit_bytes=32 << 20),
    )(
        samples,
        jnp.asarray(dft_table()),
        live.reshape(1, CH),
        live.reshape(CH, 1),
        jnp.asarray(inverse_counts()),
    )


def exchange_kernel(
    white_ref,
    power_ref,
    bands_ref,
    weights_ref,
    parts,
    own_weights,
    power_send,
    power_recv,
    weight_send,
    weight_recv,
    seg_send,
    seg_recv,
    local_sem,
    own_y_send,
    own_x_send,
    fwd_x_send,
    core_a_send,
    core_b_send,
    slot_recv,
):
    chan = lax.axis_index("chan")
    seg = lax.axis_index("seg")
    y = chan // 4
    x_hi = (chan // 2) % 2
    core = chan % 2

    barrier = pltpu.get_barrier_semaphore()

    def greet(i, carry):
        pl.semaphore_signal(
            barrier, inc=1, device_id=(chan, (seg + i) % N_SEG), device_id_type=MESH
        )
        pl.semaphore_signal(
            barrier, inc=1, device_id=((chan + i) % N_CHAN, seg), device_id_type=MESH
        )
        return carry

    lax.fori_loop(1, 16, greet, 0)
    pl.semaphore_wait(barrier, 30)

    def power_copy(i):
        return pltpu.make_async_remote_copy(
            src_ref=power_ref,
            dst_ref=parts.at[chan],
            send_sem=power_send.at[i],
            recv_sem=power_recv.at[i],
            device_id=((chan + i) % N_CHAN, seg),
            device_id_type=MESH,
        )

    def seg_copy(f, i):
        target = (seg + i) % N_SEG
        return pltpu.make_async_remote_copy(
            src_ref=white_ref.at[target, f],
            dst_ref=bands_ref.at[0, f, seg],
            send_sem=seg_send.at[f, i],
            recv_sem=seg_recv.at[f, i],
            device_id=(chan, target),
            device_id_type=MESH,
        )

    def local_copy(f):
        return pltpu.make_async_copy(
            white_ref.at[seg, f], bands_ref.at[0, f, seg], local_sem.at[f]
        )

    def weight_copy(i):
        return pltpu.make_async_remote_copy(
            src_ref=own_weights,
            dst_ref=weights_ref.at[seg],
            send_sem=weight_send.at[i],
            recv_sem=weight_recv.at[i],
            device_id=(chan, (seg + i) % N_SEG),
            device_id_type=MESH,
        )

    def block_copy(source, slot, f, send, target):
        return pltpu.make_async_remote_copy(
            src_ref=bands_ref.at[source, f],
            dst_ref=bands_ref.at[slot, f],
            send_sem=send.at[f],
            recv_sem=slot_recv.at[slot, f],
            device_id=(target, seg),
            device_id_type=MESH,
        )

    def each(first, last, fn):
        def body(i, carry):
            fn(i)
            return carry

        lax.fori_loop(first, last, body, 0)

    each(1, 16, lambda i: power_copy(i).start())
    for f in range(BAND):
        each(1, 16, lambda i: seg_copy(f, i).start())
        local_copy(f).start()

    parts[chan] = power_ref[...]
    each(1, 16, lambda i: power_copy(i).wait())
    total = jnp.sum(parts[...], axis=0)
    lane = lax.broadcasted_iota(jnp.int32, (1, 128), 1)
    weights = 1.0 / jnp.sqrt(total / (CHANNELS * L) + eps_power)
    weights = jnp.where(lane < SEG_DEV, weights, 0.0)
    own_weights[...] = weights
    weights_ref[seg] = weights
    each(1, 16, lambda i: weight_copy(i).start())

    other = chan + 1 - 2 * core
    own_y = functools.partial(block_copy, 0, 4, send=own_y_send, target=(chan + 12) % 16)
    own_x = functools.partial(block_copy, 0, 2, send=own_x_send, target=chan // 4 * 4 + core)
    fwd_x = functools.partial(block_copy, 4, 2, send=fwd_x_send, target=chan // 4 * 4 + 2 + core)
    even_a = functools.partial(block_copy, 2, 1, send=core_a_send, target=other)
    even_b = functools.partial(block_copy, 4, 3, send=core_b_send, target=other)
    odd_a = functools.partial(block_copy, 0, 1, send=core_a_send, target=other)
    odd_b = functools.partial(block_copy, 2, 3, send=core_b_send, target=other)

    has_near = jnp.logical_or(y < 3, x_hi == 0)
    has_far = y < 3

    def arrived(slot, f):
        block_copy(0, slot, f, own_y_send, chan).wait_recv()

    def send_own(f):
        @pl.when(y > 0)
        def _():
            own_y(f=f).start()

        @pl.when(x_hi == 1)
        def _():
            own_x(f=f).start()

        @pl.when(core == 1)
        def _():
            odd_a(f=f).start()

    def forward_far(f):
        @pl.when(has_far)
        def _():
            arrived(4, f)

            @pl.when(x_hi == 0)
            def _():
                fwd_x(f=f).start()

            @pl.when(core == 0)
            def _():
                even_b(f=f).start()

    def forward_near(f):
        @pl.when(has_near)
        def _():
            arrived(2, f)

            @pl.when(core == 0)
            def _():
                even_a(f=f).start()

            @pl.when(core == 1)
            def _():
                odd_b(f=f).start()

    for f in range(BAND):
        local_copy(f).wait()
        each(1, 16, lambda i: seg_copy(f, i).wait_recv())
        send_own(f)
        if f > 0:
            forward_far(f - 1)
        if f > 1:
            forward_near(f - 2)
    forward_far(BAND - 1)
    forward_near(BAND - 2)
    forward_near(BAND - 1)

    for f in range(BAND):

        @pl.when(jnp.logical_or(core == 0, has_near))
        def _():
            arrived(1, f)

        @pl.when(jnp.logical_or(jnp.logical_and(core == 0, has_near), has_far))
        def _():
            arrived(3, f)

        each(1, 16, lambda i: seg_copy(f, i).wait_send())

        @pl.when(y > 0)
        def _():
            own_y(f=f).wait_send()

        @pl.when(x_hi == 1)
        def _():
            own_x(f=f).wait_send()

        @pl.when(jnp.logical_and(has_far, x_hi == 0))
        def _():
            fwd_x(f=f).wait_send()

        @pl.when(jnp.logical_or(core == 1, has_near))
        def _():
            even_a(f=f).wait_send()

        @pl.when(jnp.logical_or(jnp.logical_and(core == 1, has_near), jnp.logical_and(core == 0, has_far)))
        def _():
            even_b(f=f).wait_send()

    each(1, 16, lambda i: weight_copy(i).wait())


def exchange(white, power):
    dma = pltpu.SemaphoreType.DMA
    return pl.pallas_call(
        exchange_kernel,
        out_shape=(
            jax.ShapeDtypeStruct((NEAR, BAND, N_SEG, 2 * SEG_PAD, CH), jnp.bfloat16),
            jax.ShapeDtypeStruct((N_SEG, 1, 128), jnp.float32),
        ),
        in_specs=[pl.BlockSpec(memory_space=pltpu.VMEM)] * 2,
        out_specs=(
            pl.BlockSpec(memory_space=pl.ANY),
            pl.BlockSpec(memory_space=pltpu.VMEM),
        ),
        scratch_shapes=[
            pltpu.VMEM((N_CHAN, 1, 128), jnp.float32),
            pltpu.VMEM((1, 128), jnp.float32),
            dma((16,)),
            dma((16,)),
            dma((16,)),
            dma((16,)),
            dma((BAND, 16)),
            dma((BAND, 16)),
            dma((BAND,)),
            dma((BAND,)),
            dma((BAND,)),
            dma((BAND,)),
            dma((BAND,)),
            dma((BAND,)),
            dma((NEAR, BAND)),
        ],
        compiler_params=pltpu.CompilerParams(
            collective_id=0, has_side_effects=True, vmem_limit_bytes=32 << 20
        ),
    )(white, power)


def cross_kernel(chan_ref, bands_ref, weights_ref, out_ref, left):
    lane = lax.broadcasted_iota(jnp.int32, (SEG_PAD, 128), 1)
    row = lax.broadcasted_iota(jnp.int32, (SEG_PAD, 128), 0)
    factor = math.sqrt(SEGMENTS) / jnp.sum(weights_ref[...])
    for source in range(N_SEG):
        spread = jnp.broadcast_to(weights_ref[source], (SEG_PAD, 128))
        scale = jnp.sum(jnp.where(lane == row, spread, 0.0), axis=1, keepdims=True) * factor
        real = bands_ref[0, 0, source, :SEG_PAD, :].astype(jnp.float32) * scale
        imag = bands_ref[0, 0, source, SEG_PAD:, :].astype(jnp.float32) * scale
        first = source * 2 * SEG_PAD
        left[0, first : first + SEG_PAD, :] = real.astype(jnp.bfloat16)
        left[0, first + SEG_PAD : first + 2 * SEG_PAD, :] = imag.astype(jnp.bfloat16)
        left[1, first : first + SEG_PAD, :] = (-imag).astype(jnp.bfloat16)
        left[1, first + SEG_PAD : first + 2 * SEG_PAD, :] = real.astype(jnp.bfloat16)
    block = chan_ref[0]
    mine = lax.broadcasted_iota(jnp.int32, (CH, CH), 0)
    theirs = lax.broadcasted_iota(jnp.int32, (CH, CH), 1)
    for r in range(2):
        rows = left[r].T
        for k in range(NEAR):
            partner = bands_ref[k, 0].reshape(N_SEG * 2 * SEG_PAD, CH)
            product = jnp.dot(rows, partner, preferred_element_type=jnp.float32)
            keep = block + k < N_CHAN
            if k == 0:
                keep = jnp.logical_and(keep, theirs > mine)
            if k == REACH:
                keep = jnp.logical_and(keep, theirs <= mine)
            product = jnp.where(keep, product, 0.0)
            out_ref[0, k, :, r * CH : (r + 1) * CH] = product.astype(jnp.bfloat16)


def cross(chan, bands, weights):
    return pl.pallas_call(
        cross_kernel,
        grid=(BAND,),
        out_shape=jax.ShapeDtypeStruct((BAND, NEAR, CH, 2 * CH), jnp.bfloat16),
        in_specs=[
            pl.BlockSpec(memory_space=pltpu.SMEM),
            pl.BlockSpec((NEAR, 1, N_SEG, 2 * SEG_PAD, CH), lambda f: (0, f, 0, 0, 0)),
            pl.BlockSpec((N_SEG, 1, 128), lambda f: (0, 0, 0)),
        ],
        out_specs=pl.BlockSpec((1, NEAR, CH, 2 * CH), lambda f: (f, 0, 0, 0)),
        scratch_shapes=[pltpu.VMEM((2, N_SEG * 2 * SEG_PAD, CH), jnp.bfloat16)],
        compiler_params=pltpu.CompilerParams(vmem_limit_bytes=32 << 20),
    )(chan, bands, weights)


def on_device(samples, live_trace):
    by_segment = jnp.transpose(samples, (1, 0, 2))
    live = live_trace.astype(jnp.float32)
    white, power = whiten(by_segment, live)
    bands, weights = exchange(white, power)
    chan = lax.axis_index("chan").reshape(1)
    stacked = cross(chan, bands, weights)
    return jnp.transpose(stacked, (0, 2, 1, 3))


def solution(mesh):
    in_specs = (P("chan", "seg", None), P("chan"))
    out_specs = P("seg", "chan", None, None)
    return jax.shard_map(
        on_device, mesh=mesh, in_specs=in_specs, out_specs=out_specs, check_vma=False
    )
```

time: 187 us -> 73.3 us (0.39)
  blocking collectives: 83.5 us -> 0 us
  Pallas kernels: 0 us -> 67.3 us
  waiting for transfers between devices: 35.6 us -> 0 us
  starting transfers between devices: 22.4 us -> 0 us
  other arithmetic: 18.5 us -> 0.68 us
  matrix products: 15.5 us -> 0 us
  local copies, waits for them, and re-layouts: 8.74 us -> 5.15 us
    pallas_call x0 -> x3, Pallas kernels: none -> 67.3 us  [the longest x1 55.5 us: exchange(): pl.pallas_call(exchange_kernel, out_shape=(jax.ShapeDtypeStruct((NEAR, BA...]
    psum x2 -> x0, blocking collectives: 56 us -> none  [the longest x1 28.7 us: on_device(): power_sum = lax.psum(local_power, 'chan')]
    ppermute x4 -> x0, waiting for transfers between devices: 35.6 us -> none  [shifted(): return lax.ppermute(block, axis, route)]
    all_to_all x1 -> x0, blocking collectives: 27.5 us -> none  [on_device(): lax.all_to_all(whitened, 'seg', split_axis=0, concat_axis=2, tiled=True)]
    ppermute x4 -> x0, starting transfers between devices: 22.4 us -> none  [shifted(): return lax.ppermute(block, axis, route)]
    dot_general x7 -> x0, matrix products: 15.5 us -> none  [the longest x5 10.5 us: cross_block(): jnp.einsum('fkc,fkm->fcm', own_rows, partner_rows, preferred_element_type...]
    convert_element_type x3 -> x1, other arithmetic: 7 us -> 0.68 us  [on_device(): live = live_trace.astype(jnp.float32)]
    dot_general x1 -> x0, other arithmetic: 4.99 us -> none  [on_device(): jnp.einsum('csl,csl->cs', samples, samples, preferred_element_type=jnp.fl...]
  transfers between devices with their start and end apart: 4 -> 0, of which waited for: 3 -> 0; matrix products, arithmetic and copies ran while one was open for 6% -> 0% of each run, Pallas kernels for 0% -> 0%
where the time goes in v1:
time: 73.3 us; the launch traced here: 73.1 us
  Pallas kernels  67.3 us (92%)
  local copies, waits for them, and re-layouts  5.15 us (7%)
    pallas_call x1, Pallas kernels, exchange(): pl.pallas_call(exchange_kernel, out_shape=(jax.ShapeDtypeStruct((NEAR, BA...  55.5 us
    pallas_call x1, Pallas kernels, cross(): pl.pallas_call(cross_kernel, grid=(BAND,), out_shape=jax.ShapeDtypeStruct...  5.9 us
    pallas_call x1, Pallas kernels, whiten(): pl.pallas_call(whiten_kernel, grid=(SEG_DEV // STEP,), out_shape=(jax.Sha...  5.81 us
    unnamed x6, local copies, waits for them, and re-layouts  5.02 us

profile of v1, /device:TPU:7, one launch (start us, length us, event | category | flops | bytes accessed | tf_op | source)
XLA Modules:
  0.0 73.1 jit_solution(11410697547313435799)
XLA Ops:
  0.0 0.7 convert_element_type.3
  0.7 0.1 copy.5.col_ref
  0.8 0.0 copy-start
  0.8 3.2 %copy-done = bf16[256,15,1024]{2,0,1:T(8,128)(2,1)S(1)} copy-done((bf16[256,15,1024]{2,0,1:T(8,128)(2,1)S(1)}, bf16[256,15,1024]{2,0,1:T(8,128)(2,1)}, u32[]{:S(2)}) %copy-start) | copy-done | bytes 7864344
  4.1 0.0 copy-start.1
  4.1 0.9 %copy-done.1 = bf16[1024,128]{1,0:T(8,128)(2,1)S(1)} copy-done((bf16[1024,128]{1,0:T(8,128)(2,1)S(1)}, bf16[1024,128]{1,0:T(8,128)(2,1)}, u32[]{:S(2)}) %copy-start.1) | copy-done | bytes 262168
  5.0 0.0 copy-start.2
  5.0 0.8 %copy-done.2 = f32[64,256]{1,0:T(8,128)S(1)} copy-done((f32[64,256]{1,0:T(8,128)S(1)}, f32[64,256]{1,0:T(8,128)}, u32[]{:S(2)}) %copy-start.2) | copy-done | bytes 65560
  5.9 5.8 %shard_map.46 = (bf16[16,4,32,256]{3,2,1,0:T(8,128)(2,1)S(1)}, f32[1,128]{1,0:T(1,128)S(1)}) custom-call(bf16[15,256,1024]{2,1,0:T(8,128)(2,1)S(1)} %bitcast.5, bf16[1024,128]{1,0:T(8,128)(2,1)S(1)} %copy-done.1, f32[1,256]{1,0:T(1,128)S(1)} %bitcast.7, f32[256,1]{1,0:T(8,128)S(1)} %copy.5.col_ref, f32[64,256]{1,0:T(8,128)S(1)} %copy-done.2), custom_call_target="tpu_custom_call" | custom-call | tf_op jit(solution)/shard_map/pallas_call | solution.py:107
  11.7 55.5 %shard_map.47 = (bf16[5,4,16,32,256]{4,3,2,1,0:T(8,128)(2,1)S(1)}, f32[16,1,128]{2,1,0:T(1,128)S(1)}) custom-call(bf16[16,4,32,256]{3,2,1,0:T(8,128)(2,1)S(1)} %get-tuple-element.9.white_ref, f32[1,128]{1,0:T(1,128)S(1)} %get-tuple-element.10.power_ref), custom_call_target="tpu_custom_call" | custom-call | tf_op jit(solution)/shard_map/pallas_call | solution.py:351
  67.2 5.9 %shard_map.48 = bf16[4,5,256,512]{3,2,1,0:T(8,128)(2,1)} custom-call(s32[1]{0:T(128)} %bitcast.chan_ref, bf16[5,4,16,32,256]{4,3,2,1,0:T(8,128)(2,1)S(1)} %get-tuple-element.11.bands_ref, f32[16,1,128]{2,1,0:T(1,128)S(1)} %get-tuple-element.12.weights_ref), custom_call_target="tpu_custom_call" | custom-call | tf_op jit(solution)/shard_map/pallas_call | solution.py:417
Async XLA Ops:
  0.8 3.2 %copy-start = (bf16[256,15,1024]{2,0,1:T(8,128)(2,1)S(1)}, bf16[256,15,1024]{2,0,1:T(8,128)(2,1)}, u32[]{:S(2)}) copy-start(bf16[256,15,1024]{2,0,1:T(8,128)(2,1)} %param.4) | copy-start | bytes 23592964
  4.1 0.9 %copy-start.1 = (bf16[1024,128]{1,0:T(8,128)(2,1)S(1)}, bf16[1024,128]{1,0:T(8,128)(2,1)}, u32[]{:S(2)}) copy-start(bf16[1024,128]{1,0:T(8,128)(2,1)} %constant.9.clone.table_ref) | copy-start | bytes 786436
  5.0 0.8 %copy-start.2 = (f32[64,256]{1,0:T(8,128)S(1)}, f32[64,256]{1,0:T(8,128)}, u32[]{:S(2)}) copy-start(f32[64,256]{1,0:T(8,128)} %constant.10.clone.count_ref) | copy-start | bytes 196612

commit v2 on v0

v2 whole, which is shorter than its diff:
```python
import functools
import math

import jax
import jax.numpy as jnp
import numpy as np
from jax import lax
from jax.experimental import pallas as pl
from jax.experimental.pallas import tpu as pltpu
from jax.sharding import PartitionSpec as P

L = 1024
F = 64
F0 = 16
REACH = 4
NEAR = 5
CH = 256
CHANNELS = 4096
SEGMENTS = 240
N_CHAN = 16
N_SEG = 16
SEG_DEV = 15
SEG_PAD = 16
HALF = 8
BAND = F // N_SEG
VMEM_LIMIT = 40 << 20
CHUNKS = ((0, 0, 2), (0, 2, 2), (1, 0, 2), (1, 2, 1), (1, 3, 1))

eps_power = 1e-06
water_level = 0.1
smooth_half = 2

MESH = pl.DeviceIdType.MESH


def dft_table():
    time_index = np.arange(L)
    bin_number = np.arange(F) + F0
    phase_step = (time_index[:, None] * bin_number[None, :] % L).astype(np.float32)
    angle = phase_step * np.float32(2.0 * math.pi / L)
    taper = np.float32(0.5) - np.float32(0.5) * np.cos(
        time_index.astype(np.float32) * np.float32(2.0 * math.pi / L)
    )
    real = taper[:, None] * np.cos(angle)
    imag = -taper[:, None] * np.sin(angle)
    return np.concatenate([real, imag], axis=1).astype(jnp.bfloat16)


def each(first, last, fn):
    def step(i, carry):
        fn(i)
        return carry

    lax.fori_loop(first, last, step, 0)


def exchange_kernel(
    samples_ref,
    table_hbm,
    live_hbm,
    bands_ref,
    weights_ref,
    live_ref,
    samples,
    table,
    live_column,
    inverse,
    padded,
    energy,
    wide,
    white,
    aside,
    power,
    parts,
    own_weights,
    load_sem,
    table_sem,
    live_sem,
    power_send,
    power_recv,
    weight_send,
    weight_recv,
    z_send,
    z_recv,
    local_sem,
    pass_send,
    pass_recv,
    y_send,
    x_send,
    cross_send,
    core_a_send,
    core_b_send,
    slot_recv,
):
    chan = lax.axis_index("chan")
    seg = lax.axis_index("seg")
    y = chan // 4
    x_hi = (chan // 2) % 2
    core = chan % 2
    x_lo = seg // 8
    z = seg % 8

    def load(j):
        return pltpu.make_async_copy(samples_ref.at[j], samples.at[j], load_sem.at[j])

    load_table = pltpu.make_async_copy(table_hbm, table, table_sem)
    load_live = pltpu.make_async_copy(live_hbm, live_ref, live_sem)
    load_live.start()
    load_table.start()
    each(0, SEG_DEV, lambda j: load(j).start())

    barrier = pltpu.get_barrier_semaphore()

    def greet(i):
        pl.semaphore_signal(
            barrier, inc=1, device_id=(chan, (seg + i) % N_SEG), device_id_type=MESH
        )
        pl.semaphore_signal(
            barrier, inc=1, device_id=((chan + i) % N_CHAN, seg), device_id_type=MESH
        )

    each(1, 16, greet)
    pl.semaphore_signal(
        barrier,
        inc=1,
        device_id=(chan + 2 - 4 * x_hi, (1 - x_lo) * 8 + z),
        device_id_type=MESH,
    )

    load_live.wait()
    live_row = live_ref[...].astype(jnp.float32)
    live_column[...] = jnp.broadcast_to(live_row, (128, CH)).T
    bins = lax.broadcasted_iota(jnp.int32, (F, CH), 0)
    count = jnp.minimum(bins, smooth_half) + jnp.minimum(F - 1 - bins, smooth_half) + 1
    inverse[...] = 1.0 / count.astype(jnp.float32)
    padded[...] = jnp.zeros_like(padded)
    energy[...] = jnp.zeros_like(energy)
    for half in range(2):
        wide[1, half, (HALF - 1) * 2 * F :, :] = jnp.zeros((2 * F, 128), jnp.float32)
    load_table.wait()

    def whiten(j, slot):
        x = samples[j]
        spectra = jnp.dot(x, table[...], preferred_element_type=jnp.float32)
        squares = jnp.zeros((CH, 128), jnp.float32)
        for tile in range(L // 128):
            part = x[:, tile * 128 : (tile + 1) * 128].astype(jnp.float32)
            squares += part * part
        energy[j] = jnp.sum(squares * live_column[...], axis=0, keepdims=True)
        spectra = spectra.T
        real = spectra[:F]
        imag = spectra[F:]
        level = real * real + imag * imag
        padded[slot, 8 : 8 + F, :] = level
        near = level
        for distance in (-2, -1, 1, 2):
            near += padded[slot, 8 + distance : 8 + distance + F, :]
        mean = jnp.sum(level, axis=0, keepdims=True) * (water_level / F)
        gain = live_row / jnp.sqrt(near * inverse[...] + mean + eps_power)
        real = real * gain
        imag = imag * gain
        base = pl.multiple_of((j % HALF) * 2 * F, 2 * F)
        for half in range(2):
            lanes = slice(half * 128, half * 128 + 128)
            wide[j // HALF, half, pl.ds(base, F), :] = real[:, lanes]
            wide[j // HALF, half, pl.ds(base + F, F), :] = imag[:, lanes]

    def whiten_pair(i):
        load(2 * i).wait()
        load(2 * i + 1).wait()
        whiten(2 * i, 0)
        whiten(2 * i + 1, 1)

    def arrange(sh, f0, nf):
        for f in range(f0, f0 + nf):
            for band in range(N_SEG):
                for half in range(2):
                    rows = [
                        wide[sh, half, pl.ds(r * F + band * BAND + f, HALF, stride=2 * F), :]
                        for r in range(2)
                    ]
                    white[sh, band, f, :, half * 128 : half * 128 + 128] = jnp.concatenate(
                        rows, axis=0
                    ).astype(jnp.bfloat16)

    def z_copy(t, i):
        sh, f0, nf = CHUNKS[t]
        target = (z + i) % 8
        keep = pltpu.make_async_remote_copy(
            src_ref=white.at[sh, x_lo * 8 + target, pl.ds(f0, nf)],
            dst_ref=bands_ref.at[0, sh, pl.ds(f0, nf), x_lo * 8 + z],
            send_sem=z_send.at[t, 0, i],
            recv_sem=z_recv.at[t, 0, i],
            device_id=(chan, x_lo * 8 + target),
            device_id_type=MESH,
        )
        hand = pltpu.make_async_remote_copy(
            src_ref=white.at[sh, (1 - x_lo) * 8 + target, pl.ds(f0, nf)],
            dst_ref=aside.at[sh, pl.ds(f0, nf), z],
            send_sem=z_send.at[t, 1, i],
            recv_sem=z_recv.at[t, 1, i],
            device_id=(chan, x_lo * 8 + target),
            device_id_type=MESH,
        )
        return keep, hand

    def local_copy(t):
        sh, f0, nf = CHUNKS[t]
        keep = pltpu.make_async_copy(
            white.at[sh, x_lo * 8 + z, pl.ds(f0, nf)],
            bands_ref.at[0, sh, pl.ds(f0, nf), x_lo * 8 + z],
            local_sem.at[t, 0],
        )
        hand = pltpu.make_async_copy(
            white.at[sh, (1 - x_lo) * 8 + z, pl.ds(f0, nf)],
            aside.at[sh, pl.ds(f0, nf), z],
            local_sem.at[t, 1],
        )
        return keep, hand

    def send_chunk(t):
        def one(i):
            for copy in z_copy(t, i):
                copy.start()

        each(1, 8, one)
        for copy in local_copy(t):
            copy.start()

    def part_of(slot, t, side):
        sh, f0, nf = CHUNKS[t]
        return bands_ref.at[slot, sh, pl.ds(f0, nf), pl.ds(side * 8, 8)]

    def block_copy(source, slot, send, target, t, side, part):
        return pltpu.make_async_remote_copy(
            src_ref=part_of(source, t, side),
            dst_ref=part_of(slot, t, side),
            send_sem=send.at[t, part],
            recv_sem=slot_recv.at[slot, t, part],
            device_id=(target, seg),
            device_id_type=MESH,
        )

    def aside_copy(t, slot, send, recv, target):
        sh, f0, nf = CHUNKS[t]
        return pltpu.make_async_remote_copy(
            src_ref=aside.at[sh, pl.ds(f0, nf)],
            dst_ref=part_of(slot, t, x_lo),
            send_sem=send,
            recv_sem=recv,
            device_id=(target, (1 - x_lo) * 8 + z),
            device_id_type=MESH,
        )

    def side_of(part):
        return x_lo if part == 0 else 1 - x_lo

    def pass_copy(t):
        return aside_copy(t, 0, pass_send.at[t], pass_recv.at[t], chan)

    def cross_own(t):
        return block_copy(0, 2, cross_send, chan // 4 * 4 + core, t, x_lo, 0)

    def cross_other(t):
        return aside_copy(
            t, 2, cross_send.at[t, 1], slot_recv.at[2, t, 1], chan // 4 * 4 + core
        )

    def down_copy(t, part):
        return block_copy(0, 4, y_send, (chan + 12) % 16, t, side_of(part), part)

    def forward_copy(t, part):
        return block_copy(4, 2, x_send, chan // 4 * 4 + 2 + core, t, side_of(part), part)

    other = chan + 1 - 2 * core

    def core_copy(source, slot, t, part):
        send = core_a_send if slot == 1 else core_b_send
        return block_copy(source, slot, send, other, t, side_of(part), part)

    def arrived(slot, t, part):
        block_copy(0, slot, y_send, other, t, side_of(part), part).wait_recv()

    has_near = jnp.logical_or(y < 3, x_hi == 0)
    has_far = y < 3

    def send_own(t, part):
        @pl.when(y > 0)
        def _():
            down_copy(t, part).start()

        @pl.when(core == 1)
        def _():
            core_copy(0, 1, t, part).start()

    def after_z(t):
        def one(i):
            for copy in z_copy(t, i):
                copy.wait_recv()

        each(1, 8, one)
        for copy in local_copy(t):
            copy.wait()
        pass_copy(t).start()
        send_own(t, 0)

        @pl.when(x_hi == 1)
        def _():
            cross_other(t).start()
            cross_own(t).start()

    def after_pass(t):
        pass_copy(t).wait_recv()
        send_own(t, 1)

    def after_far(t):
        @pl.when(has_far)
        def _():
            for part in range(2):
                arrived(4, t, part)

                @pl.when(x_hi == 0)
                def _():
                    forward_copy(t, part).start()

                @pl.when(core == 0)
                def _():
                    core_copy(4, 3, t, part).start()

    def after_near(t):
        @pl.when(has_near)
        def _():
            for part in range(2):
                arrived(2, t, part)

                @pl.when(core == 0)
                def _():
                    core_copy(2, 1, t, part).start()

                @pl.when(core == 1)
                def _():
                    core_copy(2, 3, t, part).start()

    def power_copy(i):
        return pltpu.make_async_remote_copy(
            src_ref=power,
            dst_ref=parts.at[chan],
            send_sem=power_send.at[i],
            recv_sem=power_recv.at[i],
            device_id=((chan + i) % N_CHAN, seg),
            device_id_type=MESH,
        )

    def weight_copy(i):
        return pltpu.make_async_remote_copy(
            src_ref=own_weights,
            dst_ref=weights_ref.at[seg],
            send_sem=weight_send.at[i],
            recv_sem=weight_recv.at[i],
            device_id=(chan, (seg + i) % N_SEG),
            device_id_type=MESH,
        )

    each(0, HALF // 2, whiten_pair)
    first = True
    for t, chunk in enumerate(CHUNKS):
        if chunk[0] == 0:
            arrange(*chunk)
            if first:
                pl.semaphore_wait(barrier, 31)
                first = False
            send_chunk(t)
    each(HALF // 2, HALF - 1, whiten_pair)
    load(SEG_DEV - 1).wait()
    whiten(SEG_DEV - 1, 0)
    for t, chunk in enumerate(CHUNKS):
        if chunk[0] == 1:
            arrange(*chunk)
            send_chunk(t)

    lane = lax.broadcasted_iota(jnp.int32, (SEG_PAD, 1, 128), 2)
    row = lax.broadcasted_iota(jnp.int32, (SEG_PAD, 1, 128), 0)
    totals = jnp.sum(energy[...], axis=2, keepdims=True)
    power[...] = jnp.sum(jnp.where(lane == row, totals, 0.0), axis=0)
    each(1, 16, lambda i: power_copy(i).start())
    parts[chan] = power[...]
    each(1, 16, lambda i: power_copy(i).wait())
    total = jnp.sum(parts[...], axis=0)
    lane = lax.broadcasted_iota(jnp.int32, (1, 128), 1)
    weights = 1.0 / jnp.sqrt(total / (CHANNELS * L) + eps_power)
    weights = jnp.where(lane < SEG_DEV, weights, 0.0)
    own_weights[...] = weights
    weights_ref[seg] = weights
    each(1, 16, lambda i: weight_copy(i).start())

    n = len(CHUNKS)
    for step in range(n + 3):
        if step < n:
            after_z(step)
        if 0 <= step - 1 < n:
            after_pass(step - 1)
        if 0 <= step - 2 < n:
            after_far(step - 2)
        if 0 <= step - 3 < n:
            after_near(step - 3)

    for t in range(n):
        for part in range(2):

            @pl.when(jnp.logical_or(core == 0, has_near))
            def _():
                arrived(1, t, part)

            @pl.when(jnp.logical_or(jnp.logical_and(core == 0, has_near), has_far))
            def _():
                arrived(3, t, part)

    for t in range(n):

        def done(i):
            for copy in z_copy(t, i):
                copy.wait_send()

        each(1, 8, done)
        pass_copy(t).wait_send()

        @pl.when(x_hi == 1)
        def _():
            cross_other(t).wait_send()
            cross_own(t).wait_send()

        for part in range(2):

            @pl.when(y > 0)
            def _():
                down_copy(t, part).wait_send()

            @pl.when(jnp.logical_and(has_far, x_hi == 0))
            def _():
                forward_copy(t, part).wait_send()

            @pl.when(jnp.logical_or(core == 1, has_near))
            def _():
                core_copy(0, 1, t, part).wait_send()

            @pl.when(
                jnp.logical_or(
                    jnp.logical_and(core == 1, has_near), jnp.logical_and(core == 0, has_far)
                )
            )
            def _():
                core_copy(0, 3, t, part).wait_send()

    each(1, 16, lambda i: weight_copy(i).wait())


def exchange(samples, live):
    dma = pltpu.SemaphoreType.DMA
    n = len(CHUNKS)
    return pl.pallas_call(
        exchange_kernel,
        out_shape=(
            jax.ShapeDtypeStruct((NEAR, 2, BAND, N_SEG, 2 * HALF, CH), jnp.bfloat16),
            jax.ShapeDtypeStruct((N_SEG, 1, 128), jnp.float32),
        ),
        in_specs=[
            pl.BlockSpec(memory_space=pltpu.HBM),
            pl.BlockSpec(memory_space=pltpu.HBM),
            pl.BlockSpec(memory_space=pltpu.HBM),
        ],
        out_specs=(
            pl.BlockSpec(memory_space=pltpu.VMEM),
            pl.BlockSpec(memory_space=pltpu.VMEM),
        ),
        scratch_shapes=[
            pltpu.VMEM((1, CH), jnp.int32),
            pltpu.VMEM((SEG_DEV, CH, L), jnp.bfloat16),
            pltpu.VMEM((L, 2 * F), jnp.bfloat16),
            pltpu.VMEM((CH, 128), jnp.float32),
            pltpu.VMEM((F, CH), jnp.float32),
            pltpu.VMEM((2, F + 16, CH), jnp.float32),
            pltpu.VMEM((SEG_PAD, 1, 128), jnp.float32),
            pltpu.VMEM((2, 2, HALF * 2 * F, 128), jnp.float32),
            pltpu.VMEM((2, N_SEG, BAND, 2 * HALF, CH), jnp.bfloat16),
            pltpu.VMEM((2, BAND, 8, 2 * HALF, CH), jnp.bfloat16),
            pltpu.VMEM((1, 128), jnp.float32),
            pltpu.VMEM((N_CHAN, 1, 128), jnp.float32),
            pltpu.VMEM((1, 128), jnp.float32),
            dma((SEG_DEV,)),
            dma,
            dma,
            dma((16,)),
            dma((16,)),
            dma((16,)),
            dma((16,)),
            dma((n, 2, 8)),
            dma((n, 2, 8)),
            dma((n, 2)),
            dma((n,)),
            dma((n,)),
            dma((n, 2)),
            dma((n, 2)),
            dma((n, 2)),
            dma((n, 2)),
            dma((n, 2)),
            dma((NEAR, n, 2)),
        ],
        compiler_params=pltpu.CompilerParams(
            collective_id=0, has_side_effects=True, vmem_limit_bytes=VMEM_LIMIT
        ),
    )(*[
        pltpu.with_memory_space_constraint(value, pltpu.HBM)
        for value in (samples, jnp.asarray(dft_table()), live)
    ])


def cross_kernel(chan_ref, bands_ref, weights_ref, out_ref, left, result, out_sem):
    lane = lax.broadcasted_iota(jnp.int32, (HALF, 128), 1)
    row = lax.broadcasted_iota(jnp.int32, (HALF, 128), 0)
    factor = math.sqrt(SEGMENTS) / jnp.sum(weights_ref[...])
    block = chan_ref[0]
    mine = lax.broadcasted_iota(jnp.int32, (CH, CH), 0)
    theirs = lax.broadcasted_iota(jnp.int32, (CH, CH), 1)
    for f in range(BAND):
        for sh in range(2):
            for source in range(N_SEG):
                spread = jnp.broadcast_to(weights_ref[source], (HALF, 128))
                scale = jnp.where(lane == row + sh * HALF, spread, 0.0)
                scale = jnp.sum(scale, axis=1, keepdims=True) * factor
                both = bands_ref[0, sh, f, source].astype(jnp.float32)
                real = both[:HALF] * scale
                imag = both[HALF:] * scale
                first = (sh * N_SEG + source) * 2 * HALF
                rows = slice(first, first + 2 * HALF)
                left[f % 2, 0, rows, :] = jnp.concatenate([real, imag], axis=0).astype(jnp.bfloat16)
                left[f % 2, 1, rows, :] = jnp.concatenate([-imag, real], axis=0).astype(jnp.bfloat16)
        turned = [left[f % 2, r].T for r in range(2)]
        for k in range(NEAR):
            for r in range(2):
                product = jnp.zeros((CH, CH), jnp.float32)
                for sh in range(2):
                    partner = bands_ref[k, sh, f].reshape(CH, CH)
                    product += jnp.dot(
                        turned[r][:, sh * CH : (sh + 1) * CH],
                        partner,
                        preferred_element_type=jnp.float32,
                    )
                keep = block + k < N_CHAN
                if k == 0:
                    keep = jnp.logical_and(keep, theirs > mine)
                if k == REACH:
                    keep = jnp.logical_and(keep, theirs <= mine)
                product = jnp.where(keep, product, 0.0)
                result[f, k, :, r * CH : (r + 1) * CH] = product.astype(jnp.bfloat16)
            pltpu.make_async_copy(result.at[f, k], out_ref.at[f, k], out_sem.at[f, k]).start()
    for f in range(BAND):
        for k in range(NEAR):
            pltpu.make_async_copy(result.at[f, k], out_ref.at[f, k], out_sem.at[f, k]).wait()


def cross(chan, bands, weights):
    return pl.pallas_call(
        cross_kernel,
        out_shape=jax.ShapeDtypeStruct((BAND, NEAR, CH, 2 * CH), jnp.bfloat16),
        in_specs=[
            pl.BlockSpec(memory_space=pltpu.SMEM),
            pl.BlockSpec(memory_space=pltpu.VMEM),
            pl.BlockSpec(memory_space=pltpu.VMEM),
        ],
        out_specs=pl.BlockSpec(memory_space=pltpu.HBM),
        scratch_shapes=[
            pltpu.VMEM((2, 2, N_SEG * 2 * SEG_PAD, CH), jnp.bfloat16),
            pltpu.VMEM((BAND, NEAR, CH, 2 * CH), jnp.bfloat16),
            pltpu.SemaphoreType.DMA((BAND, NEAR)),
        ],
        compiler_params=pltpu.CompilerParams(vmem_limit_bytes=40 << 20),
    )(chan, bands, weights)


def on_device(samples, live_trace):
    by_segment = jnp.transpose(samples, (1, 0, 2))
    bands, weights = exchange(by_segment, live_trace.reshape(1, CH))
    chan = lax.axis_index("chan").reshape(1)
    stacked = cross(chan, bands, weights)
    return jnp.transpose(stacked, (0, 2, 1, 3))


def solution(mesh):
    in_specs = (P("chan", "seg", None), P("chan"))
    out_specs = P("seg", "chan", None, None)
    return jax.shard_map(
        on_device, mesh=mesh, in_specs=in_specs, out_specs=out_specs, check_vma=False
    )
```

time: 187 us -> 68.8 us (0.37)
  blocking collectives: 83.5 us -> 0 us
  Pallas kernels: 0 us -> 68.7 us
  waiting for transfers between devices: 35.6 us -> 0 us
  starting transfers between devices: 22.4 us -> 0 us
  other arithmetic: 18.5 us -> 0 us
  matrix products: 15.5 us -> 0 us
  local copies, waits for them, and re-layouts: 8.74 us -> 0 us
    pallas_call x0 -> x2, Pallas kernels: none -> 68.7 us  [the longest x1 64.7 us: exchange(): pl.pallas_call(exchange_kernel, out_shape=(jax.ShapeDtypeStruct((NEAR, 2,...]
    psum x2 -> x0, blocking collectives: 56 us -> none  [the longest x1 28.7 us: on_device(): power_sum = lax.psum(local_power, 'chan')]
    ppermute x4 -> x0, waiting for transfers between devices: 35.6 us -> none  [shifted(): return lax.ppermute(block, axis, route)]
    all_to_all x1 -> x0, blocking collectives: 27.5 us -> none  [on_device(): lax.all_to_all(whitened, 'seg', split_axis=0, concat_axis=2, tiled=True)]
    ppermute x4 -> x0, starting transfers between devices: 22.4 us -> none  [shifted(): return lax.ppermute(block, axis, route)]
    dot_general x7 -> x0, matrix products: 15.5 us -> none  [the longest x5 10.5 us: cross_block(): jnp.einsum('fkc,fkm->fcm', own_rows, partner_rows, preferred_element_type...]
    convert_element_type x3 -> x0, other arithmetic: 7 us -> none  [the longest x1 6.64 us: on_device(): return (combined * (factor * pair_mask)[None]).astype(jnp.bfloat16)]
    dot_general x1 -> x0, other arithmetic: 4.99 us -> none  [on_device(): jnp.einsum('csl,csl->cs', samples, samples, preferred_element_type=jnp.fl...]
  transfers between devices with their start and end apart: 4 -> 0, of which waited for: 3 -> 0; matrix products, arithmetic and copies ran while one was open for 6% -> 0% of each run, Pallas kernels for 0% -> 0%
where the time goes in v2:
time: 68.8 us; the launch traced here: 68.7 us
  Pallas kernels  68.7 us (100%)
    pallas_call x1, Pallas kernels, exchange(): pl.pallas_call(exchange_kernel, out_shape=(jax.ShapeDtypeStruct((NEAR, 2,...  64.7 us
    pallas_call x1, Pallas kernels, cross(): pl.pallas_call(cross_kernel, out_shape=jax.ShapeDtypeStruct((BAND, NEAR,...  4.02 us

profile of v2, /device:TPU:7, one launch (start us, length us, event | category | flops | bytes accessed | tf_op | source)
XLA Modules:
  0.0 68.7 jit_solution(7925260796393968088)
XLA Ops:
  0.0 64.7 %shard_map.37 = (bf16[5,2,4,16,16,256]{5,4,3,2,1,0:T(8,128)(2,1)S(1)}, f32[16,1,128]{2,1,0:T(1,128)S(1)}) custom-call(bf16[15,256,1024]{2,1,0:T(8,128)(2,1)} %bitcast.4, bf16[1024,128]{1,0:T(8,128)(2,1)} %constant.7.clone.table_hbm, s32[1,256]{1,0:T(1,128)} %bitcast.5), custom_call_target="tpu_custom_call" | custom-call | tf_op jit(solution)/shard_map/pallas_call | solution.py:460
  64.7 4.0 %shard_map.38 = bf16[4,5,256,512]{3,2,1,0:T(8,128)(2,1)} custom-call(s32[1]{0:T(128)} %bitcast.chan_ref, bf16[5,2,4,16,16,256]{5,4,3,2,1,0:T(8,128)(2,1)S(1)} %get-tuple-element.7.bands_ref, f32[16,1,128]{2,1,0:T(1,128)S(1)} %get-tuple-element.8.weights_ref), custom_call_target="tpu_custom_call" | custom-call | tf_op jit(solution)/shard_map/pallas_call | solution.py:562

commit v3 on v2

--- a/solution.py
+++ b/solution.py
@@ -23,8 +23,10 @@
 SEG_PAD = 16
 HALF = 8
 BAND = F // N_SEG
+GROUP = 4
+DIRECT = (1, 3, 5, 6, 7)
 VMEM_LIMIT = 40 << 20
-CHUNKS = ((0, 0, 2), (0, 2, 2), (1, 0, 2), (1, 2, 1), (1, 3, 1))
+CHUNKS = tuple((t // 4, t % 4, 1) for t in range(8))
 
 eps_power = 1e-06
 water_level = 0.1
@@ -70,6 +72,7 @@
     wide,
     white,
     aside,
+    far_aside,
     power,
     parts,
     own_weights,
@@ -82,7 +85,6 @@
     weight_recv,
     z_send,
     z_recv,
-    local_sem,
     pass_send,
     pass_recv,
     y_send,
@@ -91,6 +93,8 @@
     core_a_send,
     core_b_send,
     slot_recv,
+    aside_send,
+    aside_recv,
 ):
     chan = lax.axis_index("chan")
     seg = lax.axis_index("seg")
@@ -134,9 +138,7 @@
     count = jnp.minimum(bins, smooth_half) + jnp.minimum(F - 1 - bins, smooth_half) + 1
     inverse[...] = 1.0 / count.astype(jnp.float32)
     padded[...] = jnp.zeros_like(padded)
-    energy[...] = jnp.zeros_like(energy)
-    for half in range(2):
-        wide[1, half, (HALF - 1) * 2 * F :, :] = jnp.zeros((2 * F, 128), jnp.float32)
+    samples[SEG_DEV] = jnp.zeros((CH, L), jnp.bfloat16)
     load_table.wait()
 
     def whiten(j, slot):
@@ -165,11 +167,16 @@
             wide[j // HALF, half, pl.ds(base, F), :] = real[:, lanes]
             wide[j // HALF, half, pl.ds(base + F, F), :] = imag[:, lanes]
 
-    def whiten_pair(i):
-        load(2 * i).wait()
-        load(2 * i + 1).wait()
-        whiten(2 * i, 0)
-        whiten(2 * i + 1, 1)
+    def whiten_group(i):
+        for slot in range(GROUP - 1):
+            load(GROUP * i + slot).wait()
+
+        @pl.when(GROUP * i + GROUP - 1 < SEG_DEV)
+        def _():
+            load(GROUP * i + GROUP - 1).wait()
+
+        for slot in range(GROUP):
+            whiten(GROUP * i + slot, slot)
 
     def arrange(sh, f0, nf):
         for f in range(f0, f0 + nf):
@@ -189,16 +196,16 @@
         keep = pltpu.make_async_remote_copy(
             src_ref=white.at[sh, x_lo * 8 + target, pl.ds(f0, nf)],
             dst_ref=bands_ref.at[0, sh, pl.ds(f0, nf), x_lo * 8 + z],
-            send_sem=z_send.at[t, 0, i],
-            recv_sem=z_recv.at[t, 0, i],
+            send_sem=z_send.at[t, 0],
+            recv_sem=z_recv.at[t, 0],
             device_id=(chan, x_lo * 8 + target),
             device_id_type=MESH,
         )
         hand = pltpu.make_async_remote_copy(
             src_ref=white.at[sh, (1 - x_lo) * 8 + target, pl.ds(f0, nf)],
             dst_ref=aside.at[sh, pl.ds(f0, nf), z],
-            send_sem=z_send.at[t, 1, i],
-            recv_sem=z_recv.at[t, 1, i],
+            send_sem=z_send.at[t, 1],
+            recv_sem=z_recv.at[t, 1],
             device_id=(chan, x_lo * 8 + target),
             device_id_type=MESH,
         )
@@ -209,14 +216,27 @@
         keep = pltpu.make_async_copy(
             white.at[sh, x_lo * 8 + z, pl.ds(f0, nf)],
             bands_ref.at[0, sh, pl.ds(f0, nf), x_lo * 8 + z],
-            local_sem.at[t, 0],
+            z_recv.at[t, 0],
         )
         hand = pltpu.make_async_copy(
             white.at[sh, (1 - x_lo) * 8 + z, pl.ds(f0, nf)],
             aside.at[sh, pl.ds(f0, nf), z],
-            local_sem.at[t, 1],
+            z_recv.at[t, 1],
         )
         return keep, hand
+
+    def z_wait(t):
+        sh, f0, nf = CHUNKS[t]
+        keep = bands_ref.at[0, sh, pl.ds(f0, nf), pl.ds(x_lo * 8, 8)]
+        hand = aside.at[sh, pl.ds(f0, nf)]
+        pltpu.make_async_copy(keep, keep, z_recv.at[t, 0]).wait()
+        pltpu.make_async_copy(hand, hand, z_recv.at[t, 1]).wait()
+
+    def z_done(t):
+        sh, f0, nf = CHUNKS[t]
+        sent = aside.at[sh, pl.ds(f0, nf), pl.ds(0, 7)]
+        pltpu.make_async_copy(sent, sent, z_send.at[t, 0]).wait()
+        pltpu.make_async_copy(sent, sent, z_send.at[t, 1]).wait()
 
     def send_chunk(t):
         def one(i):
@@ -269,7 +289,28 @@
     def down_copy(t, part):
         return block_copy(0, 4, y_send, (chan + 12) % 16, t, side_of(part), part)
 
+    def aside_down(t):
+        sh, f0, nf = CHUNKS[t]
+        return pltpu.make_async_remote_copy(
+            src_ref=aside.at[sh, pl.ds(f0, nf)],
+            dst_ref=far_aside.at[sh, pl.ds(f0, nf)],
+            send_sem=aside_send.at[t],
+            recv_sem=aside_recv.at[t],
+            device_id=((chan + 12) % 16, seg),
+            device_id_type=MESH,
+        )
+
     def forward_copy(t, part):
+        sh, f0, nf = CHUNKS[t]
+        if part == 1 and t in DIRECT:
+            return pltpu.make_async_remote_copy(
+                src_ref=far_aside.at[sh, pl.ds(f0, nf)],
+                dst_ref=part_of(2, t, x_lo),
+                send_sem=x_send.at[t, 1],
+                recv_sem=slot_recv.at[2, t, 1],
+                device_id=(chan // 4 * 4 + 2 + core, (1 - x_lo) * 8 + z),
+                device_id_type=MESH,
+            )
         return block_copy(4, 2, x_send, chan // 4 * 4 + 2 + core, t, side_of(part), part)
 
     other = chan + 1 - 2 * core
@@ -294,15 +335,14 @@
             core_copy(0, 1, t, part).start()
 
     def after_z(t):
-        def one(i):
-            for copy in z_copy(t, i):
-                copy.wait_recv()
-
-        each(1, 8, one)
-        for copy in local_copy(t):
-            copy.wait()
+        z_wait(t)
         pass_copy(t).start()
         send_own(t, 0)
+        if t in DIRECT:
+
+            @pl.when(jnp.logical_and(y > 0, x_hi == 0))
+            def _():
+                aside_down(t).start()
 
         @pl.when(x_hi == 1)
         def _():
@@ -317,11 +357,20 @@
         @pl.when(has_far)
         def _():
             for part in range(2):
+                if part == 1 and t in DIRECT:
+
+                    @pl.when(x_hi == 0)
+                    def _():
+                        aside_down(t).wait_recv()
+                        forward_copy(t, part).start()
+
                 arrived(4, t, part)
 
-                @pl.when(x_hi == 0)
-                def _():
-                    forward_copy(t, part).start()
+                if part == 0 or t not in DIRECT:
+
+                    @pl.when(x_hi == 0)
+                    def _():
+                        forward_copy(t, part).start()
 
                 @pl.when(core == 0)
                 def _():
@@ -345,8 +394,8 @@
         return pltpu.make_async_remote_copy(
             src_ref=power,
             dst_ref=parts.at[chan],
-            send_sem=power_send.at[i],
-            recv_sem=power_recv.at[i],
+            send_sem=power_send,
+            recv_sem=power_recv,
             device_id=((chan + i) % N_CHAN, seg),
             device_id_type=MESH,
         )
@@ -355,13 +404,13 @@
         return pltpu.make_async_remote_copy(
             src_ref=own_weights,
             dst_ref=weights_ref.at[seg],
-            send_sem=weight_send.at[i],
-            recv_sem=weight_recv.at[i],
+            send_sem=weight_send,
+            recv_sem=weight_recv,
             device_id=(chan, (seg + i) % N_SEG),
             device_id_type=MESH,
         )
 
-    each(0, HALF // 2, whiten_pair)
+    each(0, HALF // GROUP, whiten_group)
     first = True
     for t, chunk in enumerate(CHUNKS):
         if chunk[0] == 0:
@@ -370,39 +419,42 @@
                 pl.semaphore_wait(barrier, 31)
                 first = False
             send_chunk(t)
-    each(HALF // 2, HALF - 1, whiten_pair)
-    load(SEG_DEV - 1).wait()
-    whiten(SEG_DEV - 1, 0)
-    for t, chunk in enumerate(CHUNKS):
-        if chunk[0] == 1:
-            arrange(*chunk)
-            send_chunk(t)
+    each(HALF // GROUP, SEG_PAD // GROUP, whiten_group)
 
     lane = lax.broadcasted_iota(jnp.int32, (SEG_PAD, 1, 128), 2)
     row = lax.broadcasted_iota(jnp.int32, (SEG_PAD, 1, 128), 0)
     totals = jnp.sum(energy[...], axis=2, keepdims=True)
     power[...] = jnp.sum(jnp.where(lane == row, totals, 0.0), axis=0)
     each(1, 16, lambda i: power_copy(i).start())
-    parts[chan] = power[...]
-    each(1, 16, lambda i: power_copy(i).wait())
-    total = jnp.sum(parts[...], axis=0)
-    lane = lax.broadcasted_iota(jnp.int32, (1, 128), 1)
-    weights = 1.0 / jnp.sqrt(total / (CHANNELS * L) + eps_power)
-    weights = jnp.where(lane < SEG_DEV, weights, 0.0)
-    own_weights[...] = weights
-    weights_ref[seg] = weights
-    each(1, 16, lambda i: weight_copy(i).start())
+    for t, chunk in enumerate(CHUNKS):
+        if chunk[0] == 1:
+            arrange(*chunk)
+            send_chunk(t)
+
+    def share_weights():
+        parts[chan] = power[...]
+        others = parts.at[pl.ds(0, N_CHAN - 1)]
+        pltpu.make_async_copy(others, others, power_recv).wait()
+        total = jnp.sum(parts[...], axis=0)
+        lane = lax.broadcasted_iota(jnp.int32, (1, 128), 1)
+        weights = 1.0 / jnp.sqrt(total / (CHANNELS * L) + eps_power)
+        weights = jnp.where(lane < SEG_DEV, weights, 0.0)
+        own_weights[...] = weights
+        weights_ref[seg] = weights
+        each(1, 16, lambda i: weight_copy(i).start())
 
     n = len(CHUNKS)
-    for step in range(n + 3):
+    for step in range(n + 4):
+        if step == 2:
+            share_weights()
+        if 0 <= step - 1 < n:
+            after_pass(step - 1)
         if step < n:
             after_z(step)
-        if 0 <= step - 1 < n:
-            after_pass(step - 1)
         if 0 <= step - 2 < n:
             after_far(step - 2)
-        if 0 <= step - 3 < n:
-            after_near(step - 3)
+        if 0 <= step - 4 < n:
+            after_near(step - 4)
 
     for t in range(n):
         for part in range(2):
@@ -416,18 +468,19 @@
                 arrived(3, t, part)
 
     for t in range(n):
-
-        def done(i):
-            for copy in z_copy(t, i):
-                copy.wait_send()
-
-        each(1, 8, done)
+        z_done(t)
         pass_copy(t).wait_send()
 
         @pl.when(x_hi == 1)
         def _():
             cross_other(t).wait_send()
             cross_own(t).wait_send()
+
+        if t in DIRECT:
+
+            @pl.when(jnp.logical_and(y > 0, x_hi == 0))
+            def _():
+                aside_down(t).wait_send()
 
         for part in range(2):
 
@@ -451,7 +504,9 @@
             def _():
                 core_copy(0, 3, t, part).wait_send()
 
-    each(1, 16, lambda i: weight_copy(i).wait())
+    others = weights_ref.at[pl.ds(0, N_SEG - 1)]
+    for sem in (power_send, weight_send, weight_recv):
+        pltpu.make_async_copy(others, others, sem).wait()
 
 
 def exchange(samples, live):
@@ -474,14 +529,15 @@
         ),
         scratch_shapes=[
             pltpu.VMEM((1, CH), jnp.int32),
-            pltpu.VMEM((SEG_DEV, CH, L), jnp.bfloat16),
+            pltpu.VMEM((SEG_PAD, CH, L), jnp.bfloat16),
             pltpu.VMEM((L, 2 * F), jnp.bfloat16),
             pltpu.VMEM((CH, 128), jnp.float32),
             pltpu.VMEM((F, CH), jnp.float32),
-            pltpu.VMEM((2, F + 16, CH), jnp.float32),
+            pltpu.VMEM((GROUP, F + 16, CH), jnp.float32),
             pltpu.VMEM((SEG_PAD, 1, 128), jnp.float32),
             pltpu.VMEM((2, 2, HALF * 2 * F, 128), jnp.float32),
             pltpu.VMEM((2, N_SEG, BAND, 2 * HALF, CH), jnp.bfloat16),
+            pltpu.VMEM((2, BAND, 8, 2 * HALF, CH), jnp.bfloat16),
             pltpu.VMEM((2, BAND, 8, 2 * HALF, CH), jnp.bfloat16),
             pltpu.VMEM((1, 128), jnp.float32),
             pltpu.VMEM((N_CHAN, 1, 128), jnp.float32),
@@ -489,12 +545,11 @@
             dma((SEG_DEV,)),
             dma,
             dma,
-            dma((16,)),
-            dma((16,)),
-            dma((16,)),
-            dma((16,)),
-            dma((n, 2, 8)),
-            dma((n, 2, 8)),
+            dma,
+            dma,
+            dma,
+            dma,
+            dma((n, 2)),
             dma((n, 2)),
             dma((n,)),
             dma((n,)),
@@ -504,6 +559,8 @@
             dma((n, 2)),
             dma((n, 2)),
             dma((NEAR, n, 2)),
+            dma((n,)),
+            dma((n,)),
         ],
         compiler_params=pltpu.CompilerParams(
             collective_id=0, has_side_effects=True, vmem_limit_bytes=VMEM_LIMIT

time: 68.8 us -> 58.9 us (0.86)
  Pallas kernels: 68.7 us -> 58.8 us
    pallas_call x1, Pallas kernels: 64.7 us -> 54.8 us  [exchange(): pl.pallas_call(exchange_kernel, out_shape=(jax.ShapeDtypeStruct((NEAR, 2,...]
where the time goes in v3:
time: 58.9 us; the launch traced here: 58.8 us
  Pallas kernels  58.8 us (100%)
    pallas_call x1, Pallas kernels, exchange(): pl.pallas_call(exchange_kernel, out_shape=(jax.ShapeDtypeStruct((NEAR, 2,...  54.8 us
    pallas_call x1, Pallas kernels, cross(): pl.pallas_call(cross_kernel, out_shape=jax.ShapeDtypeStruct((BAND, NEAR,...  4.02 us

profile of v3, /device:TPU:7, one launch (start us, length us, event | category | flops | bytes accessed | tf_op | source)
XLA Modules:
  0.0 58.8 jit_solution(13748061984595887498)
XLA Ops:
  0.0 54.8 %shard_map.37 = (bf16[5,2,4,16,16,256]{5,4,3,2,1,0:T(8,128)(2,1)S(1)}, f32[16,1,128]{2,1,0:T(1,128)S(1)}) custom-call(bf16[15,256,1024]{2,1,0:T(8,128)(2,1)} %bitcast.4, bf16[1024,128]{1,0:T(8,128)(2,1)} %constant.7.clone.table_hbm, s32[1,256]{1,0:T(1,128)} %bitcast.5), custom_call_target="tpu_custom_call" | custom-call | tf_op jit(solution)/shard_map/pallas_call | solution.py:515
  54.8 4.0 %shard_map.38 = bf16[4,5,256,512]{3,2,1,0:T(8,128)(2,1)} custom-call(s32[1]{0:T(128)} %bitcast.chan_ref, bf16[5,2,4,16,16,256]{5,4,3,2,1,0:T(8,128)(2,1)S(1)} %get-tuple-element.7.bands_ref, f32[16,1,128]{2,1,0:T(1,128)S(1)} %get-tuple-element.8.weights_ref), custom_call_target="tpu_custom_call" | custom-call | tf_op jit(solution)/shard_map/pallas_call | solution.py:619

commit v4 on v3

--- a/solution.py
+++ b/solution.py
@@ -575,15 +575,20 @@
     lane = lax.broadcasted_iota(jnp.int32, (HALF, 128), 1)
     row = lax.broadcasted_iota(jnp.int32, (HALF, 128), 0)
     factor = math.sqrt(SEGMENTS) / jnp.sum(weights_ref[...])
+    scales = [[], []]
+    for sh in range(2):
+        for source in range(N_SEG):
+            spread = jnp.broadcast_to(weights_ref[source] * factor, (HALF, 128))
+            scale = jnp.where(lane == row + sh * HALF, spread, 0.0)
+            scale = jnp.broadcast_to(jnp.sum(scale, axis=1, keepdims=True), (HALF, CH))
+            scales[sh].append(scale)
     block = chan_ref[0]
     mine = lax.broadcasted_iota(jnp.int32, (CH, CH), 0)
     theirs = lax.broadcasted_iota(jnp.int32, (CH, CH), 1)
     for f in range(BAND):
         for sh in range(2):
             for source in range(N_SEG):
-                spread = jnp.broadcast_to(weights_ref[source], (HALF, 128))
-                scale = jnp.where(lane == row + sh * HALF, spread, 0.0)
-                scale = jnp.sum(scale, axis=1, keepdims=True) * factor
+                scale = scales[sh][source]
                 both = bands_ref[0, sh, f, source].astype(jnp.float32)
                 real = both[:HALF] * scale
                 imag = both[HALF:] * scale

time: 58.9 us -> 58.9 us (level)
  no operation moved by 1% of the time
where the time goes in v4:
time: 58.9 us
  Pallas kernels  58.9 us (100%)
    pallas_call x1, Pallas kernels, exchange(): pl.pallas_call(exchange_kernel, out_shape=(jax.ShapeDtypeStruct((NEAR, 2,...  54.8 us
    pallas_call x1, Pallas kernels, cross(): pl.pallas_call(cross_kernel, out_shape=jax.ShapeDtypeStruct((BAND, NEAR,...  4.09 us

profile of v4, /device:TPU:7, one launch (start us, length us, event | category | flops | bytes accessed | tf_op | source)
XLA Modules:
  0.0 58.9 jit_solution(4397214791793032634)
XLA Ops:
  0.0 54.8 %shard_map.37 = (bf16[5,2,4,16,16,256]{5,4,3,2,1,0:T(8,128)(2,1)S(1)}, f32[16,1,128]{2,1,0:T(1,128)S(1)}) custom-call(bf16[15,256,1024]{2,1,0:T(8,128)(2,1)} %bitcast.4, bf16[1024,128]{1,0:T(8,128)(2,1)} %constant.7.clone.table_hbm, s32[1,256]{1,0:T(1,128)} %bitcast.5), custom_call_target="tpu_custom_call" | custom-call | tf_op jit(solution)/shard_map/pallas_call | solution.py:515
  54.8 4.1 %shard_map.38 = bf16[4,5,256,512]{3,2,1,0:T(8,128)(2,1)} custom-call(s32[1]{0:T(128)} %bitcast.chan_ref, bf16[5,2,4,16,16,256]{5,4,3,2,1,0:T(8,128)(2,1)S(1)} %get-tuple-element.7.bands_ref, f32[16,1,128]{2,1,0:T(1,128)S(1)} %get-tuple-element.8.weights_ref), custom_call_target="tpu_custom_call" | custom-call | tf_op jit(solution)/shard_map/pallas_call | solution.py:624
